TPU v7x, 32 devices: a whole 2x2x4 slice. The times are simulated.
32 devices in a mesh: groups: 2 (over y), aux: 4 (over z), ao: 2 (over x), occ: 2 (over core).
Axes of the slice: x: 2, y: 2, z: 4, core: 2. Of those that a mesh axis runs over, the one named last changes fastest.
Arguments:
- integrals: bfloat16 [16, 1024, 1536], P(('groups', 'aux'), 'ao'), parts along dimension 0, may hold values from -0.15625 to 0.15625
- coefficients: bfloat16 [2048, 2048], P(('groups', 'ao'), 'occ'), parts along dimension 0, may hold values from -6 to 6
- significant: int32 [16, 16], P(('groups', 'ao'), 'occ'), parts along dimension 0, may hold values 0 or 1
- domain: int32 [8, 16], P(('groups', 'aux'), 'occ'), parts along dimension 0, may hold values from 1 to 2
Outputs:
- exchange: float32 [2048, 1536], P(('groups', 'ao'), ('aux', 'occ')), parts along dimension 0
There are 2 independent parts, one for each index of `groups`. A program takes and returns all parts, laid end to end along the dimension named above; each array names one. Nothing has to cross between parts.
All inputs are finite; a program needn't handle non-finite values. No bound on the sum of `significant` on one device may be relied on, other than what follows from the above.
Results may differ from a plain program's by a relative error of at most 0.0011.
Values may be sent and summed in bfloat16 or wider, within the bound.
A program may use at most 64 MiB of HBM per device.

v0:
```python
import math

import jax
import jax.numpy as jnp
from jax import lax
from jax.sharding import PartitionSpec as P

TILE = 128


def with_halo(block, sides, width):
    for axis, dim in sides:
        count = lax.axis_size(axis)
        forward = [(i, i + 1) for i in range(count - 1)]
        backward = [(target, source) for source, target in forward]
        low = lax.ppermute(
            lax.slice_in_dim(block, block.shape[dim] - width, None, axis=dim), axis, forward
        )
        high = lax.ppermute(lax.slice_in_dim(block, 0, width, axis=dim), axis, backward)
        block = jnp.concatenate([low, block, high], axis=dim)
    return block


def per_device(integrals, coefficients, significant, domain):
    slab_count = integrals.shape[0]
    row_count = integrals.shape[1]
    band_width = integrals.shape[2]
    occ_count = coefficients.shape[1]
    reach = (band_width - row_count) // 2
    expanded = jnp.repeat(jnp.repeat(significant, TILE, 0), TILE, 1)
    masked = coefficients * expanded.astype(jnp.bfloat16)
    window = with_halo(masked, (("ao", 0),), reach)
    flattened = integrals.reshape(slab_count * row_count, band_width)
    product = jnp.dot(flattened, window, preferred_element_type=jnp.float32)
    product = product.reshape(slab_count, row_count, occ_count)
    limits = jnp.repeat(domain[0], TILE)
    aux_place = jnp.arange(slab_count, dtype=jnp.int32)
    retain = (aux_place[:, None] < limits[None, :]).astype(jnp.float32)
    half_form = (product * retain[:, None, :]).astype(jnp.bfloat16)
    nearby = with_halo(half_form, (("ao", 1),), reach)
    aux_devices = lax.axis_size("aux")
    occ_devices = lax.axis_size("occ")
    factor = 1.0 / math.sqrt(slab_count * aux_devices * occ_count * occ_devices)
    exchange_term = (
        lax.dot_general(
            half_form, nearby, (((0, 2), (0, 2)), ((), ())), preferred_element_type=jnp.float32
        )
        * factor
    )
    return lax.psum_scatter(exchange_term, ("aux", "occ"), scatter_dimension=1, tiled=True)


def solution(mesh):
    placed = (
        P(("groups", "aux"), "ao", None),
        P(("groups", "ao"), "occ"),
        P(("groups", "ao"), "occ"),
        P(("groups", "aux"), "occ"),
    )
    return jax.shard_map(
        per_device,
        mesh=mesh,
        in_specs=placed,
        out_specs=P(("groups", "ao"), ("aux", "occ")),
        check_vma=False,
    )
```

profile of v0, /device:TPU:0, one launch (start us, length us, event | category | flops | bytes accessed | tf_op | source)
XLA Modules:
  0.0 150.6 jit_solution(18440663706555121270)
XLA Ops:
  6.5 0.0 copy-start
  6.5 0.0 copy-start.1
  6.5 0.0 reduce-scatter.2.cloned.1.call-start
  6.5 0.8 convert_element_type.21
  7.4 0.6 broadcast_in_dim.12
  8.0 1.4 bitcast_multiply_fusion
  9.4 1.3 collective-permute-start.1
  10.7 5.0 %collective-permute-start = (bf16[512,1024]{1,0:T(8,128)(2,1)S(1)}, bf16[512,1024]{1,0:T(8,128)(2,1)S(1)}, u32[]{:S(2)}, u32[]{:S(2)}) collective-permute-start(bf16[512,1024]{1,0:T(8,128)(2,1)S(1)} %bitcast_multiply_fusion), channel_id=1, source_target_pairs={{0,2},{1,3},{4,6},{5,7},{8,10},{9,11},{12,14},{13,15},{16,18},{17,... | collective-permute-start | bytes 3145736 | tf_op jit(solution)/shard_map/ppermute | solution.py:16
  15.7 0.0 copy-done.1
  15.7 0.1 broadcast_bitcast_fusion
  15.8 21.0 %collective-permute-done.1 = bf16[512,1024]{1,0:T(8,128)(2,1)S(1)} collective-permute-done((bf16[512,1024]{1,0:T(8,128)(2,1)S(1)}, bf16[512,1024]{1,0:T(8,128)(2,1)S(1)}, u32[]{:S(2)}, u32[]{:S(2)}) %collective-permute-start.1) | collective-permute-done | bytes 1048608 | tf_op jit(solution)/shard_map/ppermute | solution.py:19
  36.8 1.2 collective-permute-done
  38.0 0.0 copy-done
  38.0 3.4 %fusion.12 = f32[1024,1024]{0,1:T(8,128)S(1)} fusion(bf16[1024,1536]{1,0:T(8,128)(2,1)S(1)} %bitcast.17, bf16[512,1024]{1,0:T(8,128)(2,1)S(1)} %collective-permute-done.1, bf16[512,1024]{1,0:T(8,128)(2,1)S(1)} %bitcast_multiply_fusion, bf16[512,1024]{1,0:T(8,128)(2,1)S(1)} %collective-permute-done), kind=kOutput, calls=%fused_computation.9 | convolution fusion | flops 3230662656 | bytes 10485760 | tf_op jit(solution)/shard_map/dot_general | solution.py:34
  41.5 0.6 multiply_convert_fusion
  42.1 1.3 collective-permute-start.3
  43.4 4.8 %collective-permute-start.2 = (bf16[2,512,1024]{2,1,0:T(8,128)(2,1)S(1)}, bf16[2,512,1024]{2,1,0:T(8,128)(2,1)S(1)}, u32[]{:S(2)}, u32[]{:S(2)}) collective-permute-start(bf16[2,512,1024]{2,1,0:T(8,128)(2,1)S(1)} %multiply_convert_fusion), channel_id=1, source_target_pairs={{0,2},{1,3},{4,6},{5,7},{8,10},{9,11},{12,14},{13,15},{16,18},{17,... | collective-permute-start | bytes 6291464 | tf_op jit(solution)/shard_map/ppermute | solution.py:16
  48.2 42.4 %collective-permute-done.3 = bf16[2,512,1024]{2,1,0:T(8,128)(2,1)S(1)} collective-permute-done((bf16[2,512,1024]{2,1,0:T(8,128)(2,1)S(1)}, bf16[2,512,1024]{2,1,0:T(8,128)(2,1)S(1)}, u32[]{:S(2)}, u32[]{:S(2)}) %collective-permute-start.3) | collective-permute-done | bytes 2097184 | tf_op jit(solution)/shard_map/ppermute | solution.py:19
  90.6 1.3 collective-permute-done.2
  91.9 8.6 %fusion.9 = f32[512,1536]{0,1:T(8,128)} fusion(bf16[2,512,1024]{2,1,0:T(8,128)(2,1)S(1)} %multiply_convert_fusion, bf16[2,512,1024]{2,1,0:T(8,128)(2,1)S(1)} %collective-permute-done.3, bf16[2,512,1024]{2,1,0:T(8,128)(2,1)S(1)} %collective-permute-done.2), kind=kOutput, calls=%fused_computation.8 | convolution fusion | flops 3240886272 | bytes 9437184 | tf_op jit(solution)/shard_map/dot_general | solution.py:45
  100.5 0.0 reduce-scatter.2.cloned.1.call-update
  100.5 43.2 %reduce-scatter.2.cloned.1.call-done = f32[512,192]{0,1:T(8,128)} async-done(((f32[512,1536]{0,1:T(8,128)}), f32[512,192]{0,1:T(8,128)}) %reduce-scatter.2.cloned.1.call-update) | async-done | bytes 393232 | tf_op jit(solution)/shard_map/reduce_scatter | solution.py:50
  (2 shorter events, 0.0 us)
Async XLA Ops:
  6.5 31.5 %copy-start = (bf16[2,512,1536]{2,1,0:T(8,128)(2,1)S(1)}, bf16[2,512,1536]{2,1,0:T(8,128)(2,1)}, u32[]{:S(2)}) copy-start(bf16[2,512,1536]{2,1,0:T(8,128)(2,1)} %param.4) | copy-start | bytes 9437188
  6.5 9.1 %copy-start.1 = (s32[1,8]{1,0:T(1,128)S(1)}, s32[1,8]{1,0:T(1,128)}, u32[]{:S(2)}) copy-start(s32[1,8]{1,0:T(1,128)} %param.7) | copy-start | bytes 100
  6.5 137.2 %reduce-scatter.2.cloned.1.call-start = ((), (), s32[]{:S(2)}) async-start(), calls=%async_computation.1 | async-start | bytes 3538944 | tf_op jit(solution)/shard_map/reduce_scatter | solution.py:50
  9.4 27.4 %collective-permute-start.1 = (bf16[512,1024]{1,0:T(8,128)(2,1)S(1)}, bf16[512,1024]{1,0:T(8,128)(2,1)S(1)}, u32[]{:S(2)}, u32[]{:S(2)}) collective-permute-start(bf16[512,1024]{1,0:T(8,128)(2,1)S(1)} %bitcast_multiply_fusion), channel_id=1, source_target_pairs={{2,0},{3,1},{6,4},{7,5},{10,8},{11,9},{14,12},{15,13},{18,16},{19,... | collective-permute-start | bytes 3145736 | tf_op jit(solution)/shard_map/ppermute | solution.py:19
  10.7 27.4 %collective-permute-start = (bf16[512,1024]{1,0:T(8,128)(2,1)S(1)}, bf16[512,1024]{1,0:T(8,128)(2,1)S(1)}, u32[]{:S(2)}, u32[]{:S(2)}) collective-permute-start(bf16[512,1024]{1,0:T(8,128)(2,1)S(1)} %bitcast_multiply_fusion), channel_id=1, source_target_pairs={{0,2},{1,3},{4,6},{5,7},{8,10},{9,11},{12,14},{13,15},{16,18},{17,... | collective-permute-start | bytes 3145736 | tf_op jit(solution)/shard_map/ppermute | solution.py:16
  42.1 48.6 %collective-permute-start.3 = (bf16[2,512,1024]{2,1,0:T(8,128)(2,1)S(1)}, bf16[2,512,1024]{2,1,0:T(8,128)(2,1)S(1)}, u32[]{:S(2)}, u32[]{:S(2)}) collective-permute-start(bf16[2,512,1024]{2,1,0:T(8,128)(2,1)S(1)} %multiply_convert_fusion), channel_id=1, source_target_pairs={{2,0},{3,1},{6,4},{7,5},{10,8},{11,9},{14,12},{15,13},{18,16},{19,... | collective-permute-start | bytes 6291464 | tf_op jit(solution)/shard_map/ppermute | solution.py:19
  43.4 48.6 %collective-permute-start.2 = (bf16[2,512,1024]{2,1,0:T(8,128)(2,1)S(1)}, bf16[2,512,1024]{2,1,0:T(8,128)(2,1)S(1)}, u32[]{:S(2)}, u32[]{:S(2)}) collective-permute-start(bf16[2,512,1024]{2,1,0:T(8,128)(2,1)S(1)} %multiply_convert_fusion), channel_id=1, source_target_pairs={{0,2},{1,3},{4,6},{5,7},{8,10},{9,11},{12,14},{13,15},{16,18},{17,... | collective-permute-start | bytes 6291464 | tf_op jit(solution)/shard_map/ppermute | solution.py:16
Sparse Core Ops, SparseCore 0:
  100.6 43.0 reduce-scatter.1
where the time goes:
time: 151 us
  waiting for transfers between devices  109 us (72%)
  between operations  13.5 us (9%)
  starting transfers between devices  12.4 us (8%)
  matrix products  12 us (8%)
  other arithmetic  2.81 us (2%)
    ppermute x2, waiting for transfers between devices, with_halo(): lax.ppermute(lax.slice_in_dim(block, 0, width, axis=dim), axis, backward)  63.5 us
    reduce_scatter x1, waiting for transfers between devices, per_device(): lax.psum_scatter(exchange_term, ('aux', 'occ'), scatter_dimension=1, tile...  43.2 us
    ppermute x2, starting transfers between devices, with_halo(): lax.ppermute(lax.slice_in_dim(block, block.shape[dim] - width, None, axis...  9.78 us
    dot_general x1, matrix products, per_device(): lax.dot_general(half_form, nearby, (((0, 2), (0, 2)), ((), ())), preferre...  8.58 us
    dot_general x1, matrix products, per_device(): product = jnp.dot(flattened, window, preferred_element_type=jnp.float32)  3.41 us
  transfers between devices with their start and end apart: 5, of which 5 were waited for; matrix products, arithmetic and copies ran while one was open for 0% of the time, Pallas kernels for 0%

commit v1 on v0

--- a/solution.py
+++ b/solution.py
@@ -1,11 +1,19 @@
+import functools
 import math
 
 import jax
 import jax.numpy as jnp
 from jax import lax
+from jax.experimental import pallas as pl
+from jax.experimental.pallas import tpu as pltpu
 from jax.sharding import PartitionSpec as P
 
 TILE = 128
+MESH = pl.DeviceIdType.MESH
+F32 = jnp.float32
+BF16 = jnp.bfloat16
+C_CHUNKS = 4
+NB = 4
 
 
 def with_halo(block, sides, width):
@@ -50,6 +58,350 @@
     return lax.psum_scatter(exchange_term, ("aux", "occ"), scatter_dimension=1, tiled=True)
 
 
+def dot_nt(a, b):
+    return lax.dot_general(a, b, (((1,), (1,)), ((), ())), preferred_element_type=F32)
+
+
+def aligned(value, unit):
+    return pl.multiple_of(value, unit)
+
+
+def pair_kernel(
+    naux, rows, occ, factor,
+    sig_ref, dom_ref, int_ref, coef_ref, out_ref,
+    craw, cw, iw, inb, acc, h, hn, kt, kc, rup, rdn, keep,
+    load_sem, c_send, c_recv, f_send, f_recv, i_send, i_recv, g_send, g_recv,
+    k_send, k_recv, up_send, up_recv, dn_send, dn_recv,
+):
+    z = lax.axis_index("aux")
+    x = lax.axis_index("ao")
+    o = lax.axis_index("occ")
+    par = lax.rem(z, 2)
+    partner = z + 1 - 2 * par
+    unit = kt.shape[1]
+    per_dev = out_ref.shape[0] // unit
+    side = rows // unit
+    crow = rows // 2 // C_CHUNKS
+    irow = rows // NB // 2
+
+    load_c = pltpu.make_async_copy(coef_ref, craw, load_sem.at[0])
+    load_c.start()
+    loads = []
+    for p in range(2):
+        load = pltpu.make_async_copy(
+            int_ref.at[p, :, pl.ds(aligned((1 - x) * rows, rows), 2 * rows)],
+            iw.at[pl.ds(p * rows, rows)],
+            load_sem.at[1 + p],
+        )
+        load.start()
+        loads.append(load)
+
+    barrier = pltpu.get_barrier_semaphore()
+    pl.semaphore_signal(barrier, inc=1, device_id={"ao": 1 - x}, device_id_type=MESH)
+    pl.semaphore_signal(barrier, inc=1, device_id={"occ": 1 - o}, device_id_type=MESH)
+
+    @pl.when(z > 0)
+    def _():
+        pl.semaphore_signal(barrier, inc=1, device_id={"aux": z - 1}, device_id_type=MESH)
+
+    @pl.when(z < naux - 1)
+    def _():
+        pl.semaphore_signal(barrier, inc=1, device_id={"aux": z + 1}, device_id_type=MESH)
+
+    block_of = lax.broadcasted_iota(jnp.int32, (1, occ), 1) // TILE
+
+    def expand(ref, row):
+        line = jnp.zeros((1, occ), F32)
+        for j in range(occ // TILE):
+            line = jnp.where(block_of == j, ref[row, j].astype(F32), line)
+        return line
+
+    limits = expand(dom_ref, 0)
+    for p in range(2):
+        keep[p : p + 1, :] = jnp.where(limits > float(p), 1.0, 0.0)
+    load_c.wait()
+    for b in range(rows // TILE):
+        mask = expand(sig_ref, b).astype(BF16)
+        cw[pl.ds(aligned(x * rows + b * TILE, TILE), TILE), :] = (
+            craw[b * TILE : (b + 1) * TILE, :] * mask
+        )
+
+    @pl.when((z > 0) & (z < naux - 1))
+    def _():
+        pl.semaphore_wait(barrier, 4)
+
+    @pl.when((z == 0) | (z == naux - 1))
+    def _():
+        pl.semaphore_wait(barrier, 3)
+
+    def c_copy(k, owner, half, send, recv, target):
+        part = cw.at[pl.ds(aligned(owner * rows + half * (rows // 2) + k * crow, crow), crow)]
+        return pltpu.make_async_remote_copy(
+            src_ref=part, dst_ref=part, send_sem=send.at[k], recv_sem=recv.at[k],
+            device_id=target, device_id_type=MESH,
+        )
+
+    def c_across(k):
+        return c_copy(k, x, par, c_send, c_recv, {"ao": 1 - x})
+
+    def c_arrival(k):
+        return c_copy(k, 1 - x, par, c_send, c_recv, {"ao": 1 - x})
+
+    def c_forward(k):
+        return c_copy(k, 1 - x, par, f_send, f_recv, {"aux": partner})
+
+    def c_forwarded(k):
+        return c_copy(k, 1 - x, 1 - par, f_send, f_recv, {"aux": partner})
+
+    for k in range(C_CHUNKS):
+        c_across(k).start()
+
+    def order(step):
+        return step + (NB - 1 - 2 * step) * (1 - x)
+
+    def i_across(step, p):
+        j = order_peer(step)
+        return pltpu.make_async_remote_copy(
+            src_ref=iw.at[pl.ds(aligned(p * rows + j * 2 * irow + o * irow, irow), irow)],
+            dst_ref=inb.at[pl.ds(aligned(step * 4 * irow + p * 2 * irow + o * irow, irow), irow)],
+            send_sem=i_send.at[step, p], recv_sem=i_recv.at[step, p],
+            device_id={"ao": 1 - x}, device_id_type=MESH,
+        )
+
+    def order_peer(step):
+        return step + (NB - 1 - 2 * step) * x
+
+    def i_core(step, p, core):
+        part = inb.at[pl.ds(aligned(step * 4 * irow + p * 2 * irow + core * irow, irow), irow)]
+        return pltpu.make_async_remote_copy(
+            src_ref=part, dst_ref=part, send_sem=g_send.at[step, p], recv_sem=g_recv.at[step, p],
+            device_id={"occ": 1 - o}, device_id_type=MESH,
+        )
+
+    for load in loads:
+        load.wait()
+
+    width = 256
+    own_rows = pl.ds(aligned(x * rows, rows), rows)
+    far_rows = pl.ds(aligned((1 - x) * rows, rows), rows)
+
+    def own_tile(t, carry):
+        cols = pl.ds(aligned(t * width, width), width)
+        acc[:, cols] = jnp.dot(iw[:, own_rows], cw[own_rows, cols], preferred_element_type=F32)
+        return carry
+
+    lax.fori_loop(0, occ // width, own_tile, 0)
+
+    for k in range(C_CHUNKS):
+        c_arrival(k).wait_recv()
+        c_forward(k).start()
+    for k in range(C_CHUNKS):
+        c_across(k).wait_send()
+    for step in range(NB):
+        for p in range(2):
+            i_across(step, p).start()
+    for k in range(C_CHUNKS):
+        c_forwarded(k).wait_recv()
+
+    def far_tile(t, carry):
+        cols = pl.ds(aligned(t * width, width), width)
+        total = acc[:, cols] + jnp.dot(
+            iw[:, far_rows], cw[far_rows, cols], preferred_element_type=F32
+        )
+        for p in range(2):
+            h[p * rows : (p + 1) * rows, cols] = (
+                total[p * rows : (p + 1) * rows] * keep[p : p + 1, cols]
+            ).astype(BF16)
+        return carry
+
+    lax.fori_loop(0, occ // width, far_tile, 0)
+
+    def core_copy(idx):
+        return pltpu.make_async_remote_copy(
+            src_ref=kt.at[idx], dst_ref=kc.at[idx], send_sem=k_send.at[idx],
+            recv_sem=k_recv.at[idx], device_id={"occ": 1 - o}, device_id_type=MESH,
+        )
+
+    def up_copy(idx):
+        return pltpu.make_async_remote_copy(
+            src_ref=kt.at[idx], dst_ref=rup.at[idx], send_sem=up_send.at[idx],
+            recv_sem=up_recv.at[idx], device_id={"aux": z + 1}, device_id_type=MESH,
+        )
+
+    def down_copy(idx):
+        return pltpu.make_async_remote_copy(
+            src_ref=kt.at[idx], dst_ref=rdn.at[idx], send_sem=dn_send.at[idx],
+            recv_sem=dn_recv.at[idx], device_id={"aux": z - 1}, device_id_type=MESH,
+        )
+
+    def place(idx):
+        owner = idx // per_dev
+        return owner // 2, lax.rem(owner, 2), lax.rem(idx, per_dev)
+
+    def share(idx):
+        _, ot, _ = place(idx)
+
+        @pl.when(ot != o)
+        def _():
+            core_copy(idx).start()
+
+    def chain(idx):
+        zt, ot, s = place(idx)
+
+        @pl.when(ot == o)
+        def _():
+            core_copy(idx).wait_recv()
+            kt[idx] = kt[idx] + kc[idx]
+
+            @pl.when((z > 0) & (z <= zt))
+            def _():
+                up_copy(idx).wait_recv()
+                kt[idx] = kt[idx] + rup[idx]
+
+            @pl.when((z < naux - 1) & (z >= zt))
+            def _():
+                down_copy(idx).wait_recv()
+                kt[idx] = kt[idx] + rdn[idx]
+
+            @pl.when(z < zt)
+            def _():
+                up_copy(idx).start()
+
+            @pl.when(z > zt)
+            def _():
+                down_copy(idx).start()
+
+            @pl.when(z == zt)
+            def _():
+                out_ref[pl.ds(aligned(s * unit, unit), unit), :] = kt[idx] * factor
+
+    def finish(idx):
+        zt, ot, _ = place(idx)
+
+        @pl.when(ot != o)
+        def _():
+            core_copy(idx).wait_send()
+
+        @pl.when((ot == o) & (z < zt))
+        def _():
+            up_copy(idx).wait_send()
+
+        @pl.when((ot == o) & (z > zt))
+        def _():
+            down_copy(idx).wait_send()
+
+    def each(first, count, body):
+        def step(n, carry):
+            body(first + n)
+            return carry
+
+        lax.fori_loop(0, count, step, 0)
+
+    out_ref[...] = jnp.zeros_like(out_ref)
+
+    def own_block(t, carry):
+        base = aligned(t * 2 * unit, 2 * unit)
+        value = dot_nt(h[pl.ds(base, 2 * unit), :], h[0:rows, :]) + dot_nt(
+            h[pl.ds(aligned(rows + base, 2 * unit), 2 * unit), :], h[rows : 2 * rows, :]
+        )
+        kt[side + 2 * t] = value[:unit]
+        kt[side + 2 * t + 1] = value[unit:]
+        share(side + 2 * t)
+        share(side + 2 * t + 1)
+        return carry
+
+    lax.fori_loop(0, side // 2, own_block, 0)
+
+    far_first = 2 * side * (1 - x)
+    per_step = side // NB
+    for step in range(NB):
+        for p in range(2):
+            i_across(step, p).wait_recv()
+            i_core(step, p, o).start()
+        if step < 2:
+            each(side + step * (side // 2), side // 2, chain)
+        else:
+            each(far_first + per_step * order(step - 2), per_step, chain)
+        for p in range(2):
+            i_core(step, p, 1 - o).wait_recv()
+        base = step * 4 * irow
+
+        def near_tile(t, carry):
+            cols = pl.ds(aligned(t * width, width), width)
+            total = jnp.dot(
+                inb[base : base + 4 * irow, :], cw[:, cols], preferred_element_type=F32
+            )
+            for p in range(2):
+                hn[p * 2 * irow : (p + 1) * 2 * irow, cols] = (
+                    total[p * 2 * irow : (p + 1) * 2 * irow] * keep[p : p + 1, cols]
+                ).astype(BF16)
+            return carry
+
+        lax.fori_loop(0, occ // width, near_tile, 0)
+        value = dot_nt(hn[0 : 2 * irow, :], h[0:rows, :]) + dot_nt(
+            hn[2 * irow : 4 * irow, :], h[rows : 2 * rows, :]
+        )
+        first = far_first + per_step * order(step)
+        for n in range(per_step):
+            kt[first + n] = value[n * unit : (n + 1) * unit]
+            share(first + n)
+    for step in (NB - 2, NB - 1):
+        each(far_first + per_step * order(step), per_step, chain)
+
+    for k in range(C_CHUNKS):
+        c_forward(k).wait_send()
+    for step in range(NB):
+        for p in range(2):
+            i_across(step, p).wait_send()
+            i_core(step, p, o).wait_send()
+    each(side, side, finish)
+    each(far_first, side, finish)
+
+
+def pair_device(naux, integrals, coefficients, significant, domain):
+    rows, band = integrals.shape[1:]
+    occ = coefficients.shape[1]
+    factor = 1.0 / math.sqrt(2 * naux * occ * 2)
+    mine = band // (2 * naux)
+    unit = 64
+    chunks = band // unit
+    dma = pltpu.SemaphoreType.DMA
+    out = pl.pallas_call(
+        functools.partial(pair_kernel, naux, rows, occ, factor),
+        out_shape=jax.ShapeDtypeStruct((mine, rows), F32),
+        in_specs=[
+            pl.BlockSpec(memory_space=pltpu.SMEM),
+            pl.BlockSpec(memory_space=pltpu.SMEM),
+            pl.BlockSpec(memory_space=pl.ANY),
+            pl.BlockSpec(memory_space=pl.ANY),
+        ],
+        out_specs=pl.BlockSpec(memory_space=pltpu.VMEM),
+        scratch_shapes=[
+            pltpu.VMEM((rows, occ), BF16),
+            pltpu.VMEM((2 * rows, occ), BF16),
+            pltpu.VMEM((2 * rows, 2 * rows), BF16),
+            pltpu.VMEM((2 * rows, 2 * rows), BF16),
+            pltpu.VMEM((2 * rows, occ), F32),
+            pltpu.VMEM((2 * rows, occ), BF16),
+            pltpu.VMEM((2 * rows // NB, occ), BF16),
+            pltpu.VMEM((chunks, unit, rows), F32),
+            pltpu.VMEM((chunks, unit, rows), F32),
+            pltpu.VMEM((chunks, unit, rows), F32),
+            pltpu.VMEM((chunks, unit, rows), F32),
+            pltpu.VMEM((2, occ), F32),
+            dma((3,)),
+            dma((C_CHUNKS,)), dma((C_CHUNKS,)), dma((C_CHUNKS,)), dma((C_CHUNKS,)),
+            dma((NB, 2)), dma((NB, 2)), dma((NB, 2)), dma((NB, 2)),
+            dma((chunks,)), dma((chunks,)), dma((chunks,)),
+            dma((chunks,)), dma((chunks,)), dma((chunks,)),
+        ],
+        compiler_params=pltpu.CompilerParams(
+            collective_id=0, has_side_effects=True, vmem_limit_bytes=48 * 1024 * 1024
+        ),
+    )(significant, domain, integrals, coefficients)
+    return out.T
+
+
 def solution(mesh):
     placed = (
         P(("groups", "aux"), "ao", None),
@@ -57,8 +409,10 @@
         P(("groups", "ao"), "occ"),
         P(("groups", "aux"), "occ"),
     )
+    two_groups = mesh.shape["ao"] == 2 and mesh.shape["aux"] == 4 and mesh.shape["occ"] == 2
+    body = functools.partial(pair_device, mesh.shape["aux"]) if two_groups else per_device
     return jax.shard_map(
-        per_device,
+        body,
         mesh=mesh,
         in_specs=placed,
         out_specs=P(("groups", "ao"), ("aux", "occ")),

time: 151 us -> 77.9 us (0.52)
  the two profiles are of different devices: /device:TPU:0 before, /device:TPU:10 now
where the time goes in v1:
time: 77.9 us; the launch traced here: 77.7 us
  Pallas kernels  72.5 us (93%)
  local copies, waits for them, and re-layouts  5.2 us (7%)
    pallas_call x1, Pallas kernels, pair_device(): pl.pallas_call(functools.partial(pair_kernel, naux, rows, occ, factor), o...  72.5 us
    unnamed x9, local copies, waits for them, and re-layouts  5.2 us

profile of v1, /device:TPU:10, one launch (start us, length us, event | category | flops | bytes accessed | tf_op | source)
XLA Modules:
  0.0 77.7 jit_solution(18028550663403478245)
XLA Ops:
  0.0 0.0 copy-start
  0.0 1.9 %copy-done = bf16[2,512,1536]{2,1,0:T(8,128)(2,1)S(1)} copy-done((bf16[2,512,1536]{2,1,0:T(8,128)(2,1)S(1)}, bf16[2,512,1536]{2,1,0:T(8,128)(2,1)}, u32[]{:S(2)}) %copy-start) | copy-done | bytes 3145752
  1.9 0.0 copy-start.1
  1.9 1.2 %copy-done.1 = bf16[512,1024]{1,0:T(8,128)(2,1)S(1)} copy-done((bf16[512,1024]{1,0:T(8,128)(2,1)S(1)}, bf16[512,1024]{1,0:T(8,128)(2,1)}, u32[]{:S(2)}) %copy-start.1) | copy-done | bytes 1048600
  3.1 0.0 copy-start.2
  3.1 0.7 copy-done.2
  3.8 0.0 copy-start.3
  3.8 0.7 copy-done.3
  4.5 72.5 %shard_map.46 = f32[192,512]{1,0:T(8,128)S(1)} custom-call(s32[4,8]{1,0:T(4,128)S(1)} %copy-done.2, s32[1,8]{1,0:T(1,128)S(1)} %copy-done.3, bf16[2,512,1536]{2,1,0:T(8,128)(2,1)S(1)} %copy-done, bf16[512,1024]{1,0:T(8,128)(2,1)S(1)} %copy-done.1), custom_call_target="tpu_custom_call" | custom-call | tf_op jit(solution)/shard_map/pallas_call | solution.py:369
  77.0 0.7 copy.6
Async XLA Ops:
  0.0 1.9 %copy-start = (bf16[2,512,1536]{2,1,0:T(8,128)(2,1)S(1)}, bf16[2,512,1536]{2,1,0:T(8,128)(2,1)}, u32[]{:S(2)}) copy-start(bf16[2,512,1536]{2,1,0:T(8,128)(2,1)} %int_ref.1) | copy-start | bytes 9437188
  1.9 1.2 %copy-start.1 = (bf16[512,1024]{1,0:T(8,128)(2,1)S(1)}, bf16[512,1024]{1,0:T(8,128)(2,1)}, u32[]{:S(2)}) copy-start(bf16[512,1024]{1,0:T(8,128)(2,1)} %coef_ref.1) | copy-start | bytes 3145732
  3.1 0.7 copy-start.2
  3.8 0.7 copy-start.3

commit v2 on v1

--- a/solution.py
+++ b/solution.py
@@ -12,7 +12,7 @@
 MESH = pl.DeviceIdType.MESH
 F32 = jnp.float32
 BF16 = jnp.bfloat16
-C_CHUNKS = 4
+C_CHUNKS = 8
 NB = 4
 
 
@@ -246,19 +246,19 @@
             core_copy(idx).start()
 
     def chain(idx):
-        zt, ot, s = place(idx)
-
-        @pl.when(ot == o)
+        zt, ot, _ = place(idx)
+
+        @pl.when((ot == o) & (z != zt))
         def _():
             core_copy(idx).wait_recv()
             kt[idx] = kt[idx] + kc[idx]
 
-            @pl.when((z > 0) & (z <= zt))
+            @pl.when((z > 0) & (z < zt))
             def _():
                 up_copy(idx).wait_recv()
                 kt[idx] = kt[idx] + rup[idx]
 
-            @pl.when((z < naux - 1) & (z >= zt))
+            @pl.when((z < naux - 1) & (z > zt))
             def _():
                 down_copy(idx).wait_recv()
                 kt[idx] = kt[idx] + rdn[idx]
@@ -271,9 +271,25 @@
             def _():
                 down_copy(idx).start()
 
-            @pl.when(z == zt)
-            def _():
-                out_ref[pl.ds(aligned(s * unit, unit), unit), :] = kt[idx] * factor
+    def arrive(idx):
+        zt, ot, s = place(idx)
+
+        @pl.when((ot == o) & (z == zt))
+        def _():
+            core_copy(idx).wait_recv()
+            kt[idx] = kt[idx] + kc[idx]
+
+            @pl.when(z > 0)
+            def _():
+                up_copy(idx).wait_recv()
+                kt[idx] = kt[idx] + rup[idx]
+
+            @pl.when(z < naux - 1)
+            def _():
+                down_copy(idx).wait_recv()
+                kt[idx] = kt[idx] + rdn[idx]
+
+            out_ref[pl.ds(aligned(s * unit, unit), unit), :] = kt[idx] * factor
 
     def finish(idx):
         zt, ot, _ = place(idx)
@@ -299,7 +315,10 @@
 
     out_ref[...] = jnp.zeros_like(out_ref)
 
-    def own_block(t, carry):
+    flip = jnp.where(z < naux // 2, 1, 0)
+
+    def own_block(n, carry):
+        t = n + flip * (side // 2 - 1 - 2 * n)
         base = aligned(t * 2 * unit, 2 * unit)
         value = dot_nt(h[pl.ds(base, 2 * unit), :], h[0:rows, :]) + dot_nt(
             h[pl.ds(aligned(rows + base, 2 * unit), 2 * unit), :], h[rows : 2 * rows, :]
@@ -311,6 +330,17 @@
         return carry
 
     lax.fori_loop(0, side // 2, own_block, 0)
+
+    def own_chain(n, carry):
+        chain(side + n + flip * (side - 1 - 2 * n))
+        return carry
+
+    def end_chain():
+        lax.fori_loop(0, side, own_chain, 0)
+
+    @pl.when((z == 0) | (z == naux - 1))
+    def _():
+        end_chain()
 
     far_first = 2 * side * (1 - x)
     per_step = side // NB
@@ -318,10 +348,6 @@
         for p in range(2):
             i_across(step, p).wait_recv()
             i_core(step, p, o).start()
-        if step < 2:
-            each(side + step * (side // 2), side // 2, chain)
-        else:
-            each(far_first + per_step * order(step - 2), per_step, chain)
         for p in range(2):
             i_core(step, p, 1 - o).wait_recv()
         base = step * 4 * irow
@@ -345,8 +371,16 @@
         for n in range(per_step):
             kt[first + n] = value[n * unit : (n + 1) * unit]
             share(first + n)
-    for step in (NB - 2, NB - 1):
-        each(far_first + per_step * order(step), per_step, chain)
+        if step == 0:
+
+            @pl.when((z > 0) & (z < naux - 1))
+            def _():
+                end_chain()
+
+        each(first, per_step, chain)
+    each(side, side, arrive)
+    for step in range(NB):
+        each(far_first + per_step * order(step), per_step, arrive)
 
     for k in range(C_CHUNKS):
         c_forward(k).wait_send()
@@ -372,8 +406,8 @@
         in_specs=[
             pl.BlockSpec(memory_space=pltpu.SMEM),
             pl.BlockSpec(memory_space=pltpu.SMEM),
-            pl.BlockSpec(memory_space=pl.ANY),
-            pl.BlockSpec(memory_space=pl.ANY),
+            pl.BlockSpec(memory_space=pltpu.HBM),
+            pl.BlockSpec(memory_space=pltpu.HBM),
         ],
         out_specs=pl.BlockSpec(memory_space=pltpu.VMEM),
         scratch_shapes=[
@@ -396,7 +430,7 @@
             dma((chunks,)), dma((chunks,)), dma((chunks,)),
         ],
         compiler_params=pltpu.CompilerParams(
-            collective_id=0, has_side_effects=True, vmem_limit_bytes=48 * 1024 * 1024
+            collective_id=0, has_side_effects=True, vmem_limit_bytes=60 * 1024 * 1024
         ),
     )(significant, domain, integrals, coefficients)
     return out.T

time: 77.9 us -> 63.1 us (0.81); the launches traced: 77.7 us -> 62.1 us
  Pallas kernels: 72.5 us -> 60.3 us
  local copies, waits for them, and re-layouts: 5.2 us -> 1.77 us
    pallas_call x1, Pallas kernels: 72.5 us -> 60.3 us  [pair_device(): pl.pallas_call(functools.partial(pair_kernel, naux, rows, occ, factor), o...]
    unnamed x9 -> x1, local copies, waits for them, and re-layouts: 5.2 us -> 1.77 us
where the time goes in v2:
time: 63.1 us; the launch traced here: 62.1 us
  Pallas kernels  60.3 us (96%)
  local copies, waits for them, and re-layouts  1.77 us (3%)
    pallas_call x1, Pallas kernels, pair_device(): pl.pallas_call(functools.partial(pair_kernel, naux, rows, occ, factor), o...  60.3 us
    unnamed x1, local copies, waits for them, and re-layouts  1.77 us

profile of v2, /device:TPU:10, one launch (start us, length us, event | category | flops | bytes accessed | tf_op | source)
XLA Modules:
  0.0 62.1 jit_solution(5667520436981974953)
XLA Ops:
  0.0 60.3 %shard_map.46 = f32[192,512]{1,0:T(8,128)} custom-call(s32[4,8]{1,0:T(4,128)} %sig_ref.1, s32[1,8]{1,0:T(1,128)} %dom_ref.1, bf16[2,512,1536]{2,1,0:T(8,128)(2,1)} %int_ref.1, bf16[512,1024]{1,0:T(8,128)(2,1)} %coef_ref.1), custom_call_target="tpu_custom_call" | custom-call | tf_op jit(solution)/shard_map/pallas_call | solution.py:403
  60.3 1.8 %copy.6 = f32[512,192]{0,1:T(8,128)} copy(f32[512,192]{0,1:T(8,128)} %bitcast.1) | data formatting | bytes 786432

commit v3 on v2

--- a/solution.py
+++ b/solution.py
@@ -58,10 +58,6 @@
     return lax.psum_scatter(exchange_term, ("aux", "occ"), scatter_dimension=1, tiled=True)
 
 
-def dot_nt(a, b):
-    return lax.dot_general(a, b, (((1,), (1,)), ((), ())), preferred_element_type=F32)
-
-
 def aligned(value, unit):
     return pl.multiple_of(value, unit)
 
@@ -69,9 +65,9 @@
 def pair_kernel(
     naux, rows, occ, factor,
     sig_ref, dom_ref, int_ref, coef_ref, out_ref,
-    craw, cw, iw, inb, acc, h, hn, kt, kc, rup, rdn, keep,
-    load_sem, c_send, c_recv, f_send, f_recv, i_send, i_recv, g_send, g_recv,
-    k_send, k_recv, up_send, up_recv, dn_send, dn_recv,
+    craw, cw, iw, inb, acc, ht, hn, kown, kt, kc, rup, rdn, kb, rb, keep, masks,
+    load_sem, m_send, m_recv, c_send, c_recv, f_send, f_recv, i_send, i_recv, g_send, g_recv,
+    ld_send, ld_recv, k_send, k_recv, up_send, up_recv, dn_send, dn_recv,
 ):
     z = lax.axis_index("aux")
     x = lax.axis_index("ao")
@@ -81,17 +77,18 @@
     unit = kt.shape[1]
     per_dev = out_ref.shape[0] // unit
     side = rows // unit
-    crow = rows // 2 // C_CHUNKS
     irow = rows // NB // 2
-
-    load_c = pltpu.make_async_copy(coef_ref, craw, load_sem.at[0])
+    width = occ // C_CHUNKS
+    own_rows = pl.ds(aligned(x * rows, rows), rows)
+    far_rows = pl.ds(aligned((1 - x) * rows, rows), rows)
+    near_cols = pl.ds(aligned((1 - x) * rows, rows), 2 * rows)
+
+    load_c = pltpu.make_async_copy(coef_ref, craw.at[own_rows], load_sem.at[0])
     load_c.start()
     loads = []
     for p in range(2):
         load = pltpu.make_async_copy(
-            int_ref.at[p, :, pl.ds(aligned((1 - x) * rows, rows), 2 * rows)],
-            iw.at[pl.ds(p * rows, rows)],
-            load_sem.at[1 + p],
+            int_ref.at[p, :, near_cols], iw.at[pl.ds(p * rows, rows)], load_sem.at[1 + p]
         )
         load.start()
         loads.append(load)
@@ -116,105 +113,137 @@
             line = jnp.where(block_of == j, ref[row, j].astype(F32), line)
         return line
 
+    blocks = rows // TILE
+    masks[x] = jnp.concatenate(
+        [expand(sig_ref, b) for b in range(blocks)] + [jnp.zeros((8 - blocks, occ), F32)], 0
+    )
+
+    @pl.when((z > 0) & (z < naux - 1))
+    def _():
+        pl.semaphore_wait(barrier, 4)
+
+    @pl.when((z == 0) | (z == naux - 1))
+    def _():
+        pl.semaphore_wait(barrier, 3)
+
+    def mask_copy(owner):
+        return pltpu.make_async_remote_copy(
+            src_ref=masks.at[owner], dst_ref=masks.at[owner], send_sem=m_send, recv_sem=m_recv,
+            device_id={"ao": 1 - x}, device_id_type=MESH,
+        )
+
+    def c_region(owner, half, k):
+        return craw.at[
+            pl.ds(aligned(owner * rows + half * (rows // 2), rows // 2), rows // 2),
+            pl.ds(k * width, width),
+        ]
+
+    def c_across(k):
+        return pltpu.make_async_remote_copy(
+            src_ref=coef_ref.at[
+                pl.ds(aligned(par * (rows // 2), rows // 2), rows // 2), pl.ds(k * width, width)
+            ],
+            dst_ref=c_region(x, par, k), send_sem=c_send.at[k], recv_sem=c_recv.at[k],
+            device_id={"ao": 1 - x}, device_id_type=MESH,
+        )
+
+    def c_arrival(k):
+        part = c_region(1 - x, par, k)
+        return pltpu.make_async_remote_copy(
+            src_ref=part, dst_ref=part, send_sem=c_send.at[k], recv_sem=c_recv.at[k],
+            device_id={"ao": 1 - x}, device_id_type=MESH,
+        )
+
+    def c_forward(k, half):
+        part = c_region(1 - x, half, k)
+        return pltpu.make_async_remote_copy(
+            src_ref=part, dst_ref=part, send_sem=f_send.at[k], recv_sem=f_recv.at[k],
+            device_id={"aux": partner}, device_id_type=MESH,
+        )
+
+    mask_copy(x).start()
+    for k in range(C_CHUNKS):
+        c_across(k).start()
+
+    def order(step):
+        return step + (NB - 1 - 2 * step) * (1 - x)
+
+    def order_peer(step):
+        return step + (NB - 1 - 2 * step) * x
+
+    def i_across(step, p):
+        j = order_peer(step)
+        return pltpu.make_async_remote_copy(
+            src_ref=int_ref.at[p, pl.ds(aligned(j * 2 * irow + o * irow, irow), irow), near_cols],
+            dst_ref=inb.at[pl.ds(aligned(step * 4 * irow + p * 2 * irow + o * irow, irow), irow)],
+            send_sem=i_send.at[step, p], recv_sem=i_recv.at[step, p],
+            device_id={"ao": 1 - x}, device_id_type=MESH,
+        )
+
+    def i_core(step, p, core):
+        part = inb.at[pl.ds(aligned(step * 4 * irow + p * 2 * irow + core * irow, irow), irow)]
+        return pltpu.make_async_remote_copy(
+            src_ref=part, dst_ref=part, send_sem=g_send.at[step, p], recv_sem=g_recv.at[step, p],
+            device_id={"occ": 1 - o}, device_id_type=MESH,
+        )
+
+    def i_begin(step):
+        for p in range(2):
+            i_across(step, p).start()
+
+    out_ref[...] = jnp.zeros_like(out_ref)
     limits = expand(dom_ref, 0)
     for p in range(2):
         keep[p : p + 1, :] = jnp.where(limits > float(p), 1.0, 0.0)
+
+    def mask_rows(owner, cols):
+        for b in range(blocks):
+            part = pl.ds(aligned(owner * rows + b * TILE, TILE), TILE)
+            cw[part, cols] = craw[part, cols] * masks[owner, b : b + 1, cols].astype(BF16)
+
     load_c.wait()
-    for b in range(rows // TILE):
-        mask = expand(sig_ref, b).astype(BF16)
-        cw[pl.ds(aligned(x * rows + b * TILE, TILE), TILE), :] = (
-            craw[b * TILE : (b + 1) * TILE, :] * mask
-        )
-
-    @pl.when((z > 0) & (z < naux - 1))
-    def _():
-        pl.semaphore_wait(barrier, 4)
-
-    @pl.when((z == 0) | (z == naux - 1))
-    def _():
-        pl.semaphore_wait(barrier, 3)
-
-    def c_copy(k, owner, half, send, recv, target):
-        part = cw.at[pl.ds(aligned(owner * rows + half * (rows // 2) + k * crow, crow), crow)]
-        return pltpu.make_async_remote_copy(
-            src_ref=part, dst_ref=part, send_sem=send.at[k], recv_sem=recv.at[k],
-            device_id=target, device_id_type=MESH,
-        )
-
-    def c_across(k):
-        return c_copy(k, x, par, c_send, c_recv, {"ao": 1 - x})
-
-    def c_arrival(k):
-        return c_copy(k, 1 - x, par, c_send, c_recv, {"ao": 1 - x})
-
-    def c_forward(k):
-        return c_copy(k, 1 - x, par, f_send, f_recv, {"aux": partner})
-
-    def c_forwarded(k):
-        return c_copy(k, 1 - x, 1 - par, f_send, f_recv, {"aux": partner})
-
-    for k in range(C_CHUNKS):
-        c_across(k).start()
-
-    def order(step):
-        return step + (NB - 1 - 2 * step) * (1 - x)
-
-    def i_across(step, p):
-        j = order_peer(step)
-        return pltpu.make_async_remote_copy(
-            src_ref=iw.at[pl.ds(aligned(p * rows + j * 2 * irow + o * irow, irow), irow)],
-            dst_ref=inb.at[pl.ds(aligned(step * 4 * irow + p * 2 * irow + o * irow, irow), irow)],
-            send_sem=i_send.at[step, p], recv_sem=i_recv.at[step, p],
-            device_id={"ao": 1 - x}, device_id_type=MESH,
-        )
-
-    def order_peer(step):
-        return step + (NB - 1 - 2 * step) * x
-
-    def i_core(step, p, core):
-        part = inb.at[pl.ds(aligned(step * 4 * irow + p * 2 * irow + core * irow, irow), irow)]
-        return pltpu.make_async_remote_copy(
-            src_ref=part, dst_ref=part, send_sem=g_send.at[step, p], recv_sem=g_recv.at[step, p],
-            device_id={"occ": 1 - o}, device_id_type=MESH,
-        )
-
+    mask_rows(x, pl.ds(0, occ))
     for load in loads:
         load.wait()
-
-    width = 256
-    own_rows = pl.ds(aligned(x * rows, rows), rows)
-    far_rows = pl.ds(aligned((1 - x) * rows, rows), rows)
+    tile = 256
 
     def own_tile(t, carry):
-        cols = pl.ds(aligned(t * width, width), width)
+        cols = pl.ds(aligned(t * tile, tile), tile)
         acc[:, cols] = jnp.dot(iw[:, own_rows], cw[own_rows, cols], preferred_element_type=F32)
         return carry
 
-    lax.fori_loop(0, occ // width, own_tile, 0)
-
+    lax.fori_loop(0, occ // tile, own_tile, 0)
+    mask_copy(1 - x).wait_recv()
+    kown[...] = jnp.zeros_like(kown)
+
+    def far_tile(k, carry):
+        cols = pl.ds(aligned(k * tile, tile), tile)
+        mask_rows(1 - x, cols)
+        total = acc[:, cols] + jnp.dot(
+            iw[:, far_rows], cw[far_rows, cols], preferred_element_type=F32
+        )
+        for p in range(2):
+            part = (total[p * rows : (p + 1) * rows] * keep[p : p + 1, cols]).astype(BF16)
+            turned = part.T
+            ht[p, cols, :] = turned
+            kown[...] += jnp.dot(part, turned, preferred_element_type=F32)
+        return carry
+
+    pieces = tile // width
     for k in range(C_CHUNKS):
         c_arrival(k).wait_recv()
-        c_forward(k).start()
-    for k in range(C_CHUNKS):
-        c_across(k).wait_send()
-    for step in range(NB):
-        for p in range(2):
-            i_across(step, p).start()
-    for k in range(C_CHUNKS):
-        c_forwarded(k).wait_recv()
-
-    def far_tile(t, carry):
-        cols = pl.ds(aligned(t * width, width), width)
-        total = acc[:, cols] + jnp.dot(
-            iw[:, far_rows], cw[far_rows, cols], preferred_element_type=F32
-        )
-        for p in range(2):
-            h[p * rows : (p + 1) * rows, cols] = (
-                total[p * rows : (p + 1) * rows] * keep[p : p + 1, cols]
-            ).astype(BF16)
-        return carry
-
-    lax.fori_loop(0, occ // width, far_tile, 0)
+        c_forward(k, par).start()
+        if k == C_CHUNKS - 2:
+            i_begin(0)
+        if k % pieces == pieces - 1 and k >= 2 * pieces - 1:
+            t = k // pieces - 1
+            for n in range(pieces):
+                c_forward(t * pieces + n, 1 - par).wait_recv()
+            far_tile(t, 0)
+    i_begin(1)
+    for n in range(pieces):
+        c_forward(C_CHUNKS - pieces + n, 1 - par).wait_recv()
+    far_tile(occ // tile - 1, 0)
 
     def core_copy(idx):
         return pltpu.make_async_remote_copy(
@@ -245,29 +274,58 @@
         def _():
             core_copy(idx).start()
 
+    lead = jnp.where(x == 0, 0, naux - 1)
+    second = jnp.where(x == 0, 1, naux - 2)
+    inward = 1 - 2 * x
+
+    def lead_copy(idx):
+        return pltpu.make_async_remote_copy(
+            src_ref=kb.at[idx], dst_ref=rb.at[idx], send_sem=ld_send.at[idx],
+            recv_sem=ld_recv.at[idx], device_id={"aux": z + inward}, device_id_type=MESH,
+        )
+
+    def lead_landed(idx):
+        return pltpu.make_async_remote_copy(
+            src_ref=kb.at[idx], dst_ref=rb.at[idx], send_sem=ld_send.at[idx],
+            recv_sem=ld_recv.at[idx], device_id={"aux": z - inward}, device_id_type=MESH,
+        )
+
+    def gather(idx, zt):
+        core_copy(idx).wait_recv()
+        kt[idx] = kt[idx] + kc[idx]
+
+        @pl.when((z > 0) & (z <= zt) & ((x == 1) | (z != second)))
+        def _():
+            up_copy(idx).wait_recv()
+            kt[idx] = kt[idx] + rup[idx]
+
+        @pl.when((z < naux - 1) & (z >= zt) & ((x == 0) | (z != second)))
+        def _():
+            down_copy(idx).wait_recv()
+            kt[idx] = kt[idx] + rdn[idx]
+
+        @pl.when((z == second) & (((x == 0) & (zt >= second)) | ((x == 1) & (zt <= second))))
+        def _():
+            lead_landed(idx).wait_recv()
+            kt[idx] = kt[idx] + rb[idx].astype(F32)
+
     def chain(idx):
         zt, ot, _ = place(idx)
 
         @pl.when((ot == o) & (z != zt))
         def _():
-            core_copy(idx).wait_recv()
-            kt[idx] = kt[idx] + kc[idx]
-
-            @pl.when((z > 0) & (z < zt))
+            gather(idx, zt)
+
+            @pl.when(z == lead)
             def _():
-                up_copy(idx).wait_recv()
-                kt[idx] = kt[idx] + rup[idx]
-
-            @pl.when((z < naux - 1) & (z > zt))
-            def _():
-                down_copy(idx).wait_recv()
-                kt[idx] = kt[idx] + rdn[idx]
-
-            @pl.when(z < zt)
+                kb[idx] = kt[idx].astype(BF16)
+                lead_copy(idx).start()
+
+            @pl.when((z < zt) & (z != lead))
             def _():
                 up_copy(idx).start()
 
-            @pl.when(z > zt)
+            @pl.when((z > zt) & (z != lead))
             def _():
                 down_copy(idx).start()
 
@@ -276,19 +334,7 @@
 
         @pl.when((ot == o) & (z == zt))
         def _():
-            core_copy(idx).wait_recv()
-            kt[idx] = kt[idx] + kc[idx]
-
-            @pl.when(z > 0)
-            def _():
-                up_copy(idx).wait_recv()
-                kt[idx] = kt[idx] + rup[idx]
-
-            @pl.when(z < naux - 1)
-            def _():
-                down_copy(idx).wait_recv()
-                kt[idx] = kt[idx] + rdn[idx]
-
+            gather(idx, zt)
             out_ref[pl.ds(aligned(s * unit, unit), unit), :] = kt[idx] * factor
 
     def finish(idx):
@@ -298,11 +344,15 @@
         def _():
             core_copy(idx).wait_send()
 
-        @pl.when((ot == o) & (z < zt))
+        @pl.when((ot == o) & (z != zt) & (z == lead))
+        def _():
+            lead_copy(idx).wait_send()
+
+        @pl.when((ot == o) & (z < zt) & (z != lead))
         def _():
             up_copy(idx).wait_send()
 
-        @pl.when((ot == o) & (z > zt))
+        @pl.when((ot == o) & (z > zt) & (z != lead))
         def _():
             down_copy(idx).wait_send()
 
@@ -318,18 +368,12 @@
     flip = jnp.where(z < naux // 2, 1, 0)
 
     def own_block(n, carry):
-        t = n + flip * (side // 2 - 1 - 2 * n)
-        base = aligned(t * 2 * unit, 2 * unit)
-        value = dot_nt(h[pl.ds(base, 2 * unit), :], h[0:rows, :]) + dot_nt(
-            h[pl.ds(aligned(rows + base, 2 * unit), 2 * unit), :], h[rows : 2 * rows, :]
-        )
-        kt[side + 2 * t] = value[:unit]
-        kt[side + 2 * t + 1] = value[unit:]
-        share(side + 2 * t)
-        share(side + 2 * t + 1)
+        t = n + flip * (side - 1 - 2 * n)
+        kt[side + t] = kown[pl.ds(aligned(t * unit, unit), unit), :]
+        share(side + t)
         return carry
 
-    lax.fori_loop(0, side // 2, own_block, 0)
+    lax.fori_loop(0, side, own_block, 0)
 
     def own_chain(n, carry):
         chain(side + n + flip * (side - 1 - 2 * n))
@@ -348,12 +392,14 @@
         for p in range(2):
             i_across(step, p).wait_recv()
             i_core(step, p, o).start()
+        if step + 2 < NB:
+            i_begin(step + 2)
         for p in range(2):
             i_core(step, p, 1 - o).wait_recv()
         base = step * 4 * irow
 
         def near_tile(t, carry):
-            cols = pl.ds(aligned(t * width, width), width)
+            cols = pl.ds(aligned(t * tile, tile), tile)
             total = jnp.dot(
                 inb[base : base + 4 * irow, :], cw[:, cols], preferred_element_type=F32
             )
@@ -363,9 +409,9 @@
                 ).astype(BF16)
             return carry
 
-        lax.fori_loop(0, occ // width, near_tile, 0)
-        value = dot_nt(hn[0 : 2 * irow, :], h[0:rows, :]) + dot_nt(
-            hn[2 * irow : 4 * irow, :], h[rows : 2 * rows, :]
+        lax.fori_loop(0, occ // tile, near_tile, 0)
+        value = jnp.dot(hn[0 : 2 * irow, :], ht[0], preferred_element_type=F32) + jnp.dot(
+            hn[2 * irow : 4 * irow, :], ht[1], preferred_element_type=F32
         )
         first = far_first + per_step * order(step)
         for n in range(per_step):
@@ -382,8 +428,10 @@
     for step in range(NB):
         each(far_first + per_step * order(step), per_step, arrive)
 
+    mask_copy(x).wait_send()
     for k in range(C_CHUNKS):
-        c_forward(k).wait_send()
+        c_across(k).wait_send()
+        c_forward(k, par).wait_send()
     for step in range(NB):
         for p in range(2):
             i_across(step, p).wait_send()
@@ -411,21 +459,26 @@
         ],
         out_specs=pl.BlockSpec(memory_space=pltpu.VMEM),
         scratch_shapes=[
-            pltpu.VMEM((rows, occ), BF16),
+            pltpu.VMEM((2 * rows, occ), BF16),
             pltpu.VMEM((2 * rows, occ), BF16),
             pltpu.VMEM((2 * rows, 2 * rows), BF16),
             pltpu.VMEM((2 * rows, 2 * rows), BF16),
             pltpu.VMEM((2 * rows, occ), F32),
-            pltpu.VMEM((2 * rows, occ), BF16),
+            pltpu.VMEM((2, occ, rows), BF16),
             pltpu.VMEM((2 * rows // NB, occ), BF16),
+            pltpu.VMEM((rows, rows), F32),
             pltpu.VMEM((chunks, unit, rows), F32),
             pltpu.VMEM((chunks, unit, rows), F32),
             pltpu.VMEM((chunks, unit, rows), F32),
             pltpu.VMEM((chunks, unit, rows), F32),
+            pltpu.VMEM((chunks, unit, rows), BF16),
+            pltpu.VMEM((chunks, unit, rows), BF16),
             pltpu.VMEM((2, occ), F32),
-            dma((3,)),
+            pltpu.VMEM((2, 8, occ), F32),
+            dma((3,)), dma, dma,
             dma((C_CHUNKS,)), dma((C_CHUNKS,)), dma((C_CHUNKS,)), dma((C_CHUNKS,)),
             dma((NB, 2)), dma((NB, 2)), dma((NB, 2)), dma((NB, 2)),
+            dma((chunks,)), dma((chunks,)),
             dma((chunks,)), dma((chunks,)), dma((chunks,)),
             dma((chunks,)), dma((chunks,)), dma((chunks,)),
         ],

time: 63.1 us -> 57 us (0.903); the launches traced: 62.1 us -> 56.8 us
  Pallas kernels: 60.3 us -> 55.1 us
    pallas_call x1, Pallas kernels: 60.3 us -> 55.1 us  [pair_device(): pl.pallas_call(functools.partial(pair_kernel, naux, rows, occ, factor), o...]
where the time goes in v3:
time: 57 us; the launch traced here: 56.8 us
  Pallas kernels  55.1 us (97%)
  local copies, waits for them, and re-layouts  1.77 us (3%)
    pallas_call x1, Pallas kernels, pair_device(): pl.pallas_call(functools.partial(pair_kernel, naux, rows, occ, factor), o...  55.1 us
    unnamed x1, local copies, waits for them, and re-layouts  1.77 us

profile of v3, /device:TPU:10, one launch (start us, length us, event | category | flops | bytes accessed | tf_op | source)
XLA Modules:
  0.0 56.8 jit_solution(4386379861516430159)
XLA Ops:
  0.0 55.1 %shard_map.46 = f32[192,512]{1,0:T(8,128)} custom-call(s32[4,8]{1,0:T(4,128)} %sig_ref.1, s32[1,8]{1,0:T(1,128)} %dom_ref.1, bf16[2,512,1536]{2,1,0:T(8,128)(2,1)} %int_ref.1, bf16[512,1024]{1,0:T(8,128)(2,1)} %coef_ref.1), custom_call_target="tpu_custom_call" | custom-call | tf_op jit(solution)/shard_map/pallas_call | solution.py:451
  55.1 1.8 %copy.6 = f32[512,192]{0,1:T(8,128)} copy(f32[512,192]{0,1:T(8,128)} %bitcast.1) | data formatting | bytes 786432
